TPU v7x, 128 devices: a whole 4x4x4 slice. The times are simulated.
128 devices in a mesh: row: 8 (over y_hi, x), col: 16 (over z, y_lo, core).
Axes of the slice: x: 4, y: 4 (y_hi: 2, y_lo: 2; y = y_hi * 2 + y_lo), z: 4, core: 2. Of those that a mesh axis runs over, the one named last changes fastest.
Arguments:
- source: float32 [32768, 128], P(('row', 'col')), may hold values from -6 to 6
- value: bfloat16 [32768, 32768], P('row', 'col'), may hold values from -128 to 127, as said below
- occupancy: int32 [256, 256], P('row', 'col'), may hold values 0 or 1
- exponent: int32 [256, 256], P('row', 'col'), may hold values from -3 to 3, as said below
Outputs:
- diffused: float32 [32768, 128], P(('row', 'col'))
Inputs may be any that keep to these rules, and one draw needn't show every extreme that they name: `value`: whole numbers, drawn independently; both ends of the range occur. `exponent`: tile exponents; every value of the range occurs.
All inputs are finite; a program needn't handle non-finite values. No bound on the sum of `occupancy` on one device may be relied on, other than what follows from the above.
Results may differ from a plain program's by a relative error of at most 0.0003.
Values sent between devices are 32-bit elements; how exact they have to be, the bound alone decides.
A program may use at most 128 MiB of HBM per device.

v0:
```python
import jax
import jax.numpy as jnp
from jax import lax
from jax.sharding import PartitionSpec as P

STEPS = 3


EPSILON = 1e-05
RETAIN = 0.8
TELEPORT = 0.2


def in_blocks(array, dim, count):
    dims = array.shape
    parts = array.reshape(*dims[:dim], count, dims[dim] // count, *dims[dim + 1 :])
    return jnp.moveaxis(parts, dim, 0)


def sum_at_owner(array, axis, dim):
    parts = in_blocks(array, dim, lax.axis_size(axis))
    arrived = lax.all_to_all(parts, axis, split_axis=0, concat_axis=0, tiled=True)
    return arrived.sum(axis=0)


def joined_along(parts, dim):
    dims = list(parts.shape[1:])
    dims[dim] *= parts.shape[0]
    return jnp.moveaxis(parts, 0, dim).reshape(dims)


def copy_for_each(array, axis):
    count = lax.axis_size(axis)
    return lax.all_to_all(
        jnp.broadcast_to(array[None], (count, *array.shape)), axis, 0, 0, tiled=True
    )


def collect(array, axis, dim):
    return joined_along(copy_for_each(array, axis), dim)


def expand_tile(value, occupancy, exponent):
    row_count = value.shape[0]
    col_count = value.shape[1]
    scales = occupancy.astype(jnp.float32) * jnp.exp2(exponent.astype(jnp.float32))
    blocked = (
        value.astype(jnp.float32).reshape(row_count // 128, 128, col_count // 128, 128)
        * scales[:, None, :, None]
    )
    return blocked.reshape(row_count, col_count).astype(jnp.bfloat16)


def shards(source, value, occupancy, exponent):
    adjacency = expand_tile(value, occupancy, exponent)
    row_count = adjacency.shape[0]
    node_count = row_count * lax.axis_size("row")
    wide_tile = adjacency.astype(jnp.float32)
    energy = sum_at_owner(jnp.sum(wide_tile * wide_tile, axis=1), "col", 0)
    inverse = 1.0 / (jnp.sqrt(node_count * 1.0) * jnp.sqrt(energy / node_count + EPSILON))
    current = source
    for iteration in range(STEPS):
        mixing = jnp.dot(
            adjacency,
            collect(current, "row", 0),
            precision=lax.Precision.HIGH,
            preferred_element_type=jnp.float32,
        )
        shares = sum_at_owner(mixing, "col", 0)
        current = jnp.tanh(RETAIN * shares * inverse[:, None] + TELEPORT * source)
    return current


def solution(mesh):
    placed = (P(("row", "col"), None), P("row", "col"), P("row", "col"), P("row", "col"))
    return jax.shard_map(
        shards, mesh=mesh, in_specs=placed, out_specs=P(("row", "col"), None), check_vma=False
    )
```

profile of v0, /device:TPU:1, one launch (start us, length us, event | category | flops | bytes accessed | tf_op | source)
XLA Modules:
  0.0 213.4 jit_solution(15395429832050756157)
XLA Ops:
  0.0 2.0 broadcast_in_dim.6
  2.0 7.5 %all-to-all-start = ((f32[8,256,128]{2,1,0:T(8,128)}), f32[8,256,128]{2,1,0:T(8,128)S(1)}, u32[]{:S(2)}, u32[]{:S(2)}) async-start(f32[8,256,128]{2,1,0:T(8,128)} %broadcast_in_dim.6), calls=%async_computation | async-start | bytes 2097152 | tf_op jit(solution)/shard_map/all_to_all | solution.py:34
  9.4 0.7 exponential_multiply_fusion
  10.2 0.1 copy.7
  10.2 2.8 %mul.60 = f32[32,128,16,128]{3,2,1,0:T(8,128)S(1)} broadcast(f32[32,16]{1,0:T(8,128)S(1)} %copy.7), dimensions={0,2} | broadcast | bytes 33556480 | tf_op jit(solution)/shard_map/mul | solution.py:48
  13.1 17.9 %multiply_reduce_fusion = (f32[4096]{0:T(1024)}, bf16[4096,2048]{1,0:T(8,128)(2,1)}) fusion(f32[512,8,16,128]{3,2,1,0:T(8,128)S(1)} %bitcast.27, bf16[4096,2048]{1,0:T(8,128)(2,1)} %param.5), kind=kLoop, calls=%fused_computation.2 | loop fusion | flops 50327552 | bytes 67125248 | tf_op jit(solution)/shard_map/reduce_sum | solution.py:59
  31.0 0.0 all-to-all-done
  31.0 6.4 %all-to-all-start.2 = ((f32[16,1,256]{2,1,0:T(1,128)}), f32[16,1,256]{2,1,0:T(1,128)S(1)}, u32[]{:S(2)}, u32[]{:S(2)}) async-start(f32[16,1,256]{2,1,0:T(1,128)} %bitcast.3), calls=%async_computation.2 | async-start | bytes 32768 | tf_op jit(solution)/shard_map/all_to_all | solution.py:22
  37.4 0.0 copy-start
  37.4 13.5 %fusion.2 = f32[16,256,128]{2,1,0:T(8,128)} fusion(bf16[16,256,2048]{2,1,0:T(8,128)(2,1)} %bitcast.24, f32[2048,128,1]{1,0,2:T(8,128)S(1)} %bitcast.28), kind=kOutput, calls=%fused_computation.8 | convolution fusion | flops 6442450944 | bytes 19922944 | tf_op jit(solution)/shard_map/dot_general | solution.py:63
  50.9 0.0 all-to-all-done.2
  50.9 5.7 %all-to-all-start.1 = ((f32[16,256,128]{2,1,0:T(8,128)}), f32[16,256,128]{2,1,0:T(8,128)S(1)}, u32[]{:S(2)}, u32[]{:S(2)}) async-start(f32[16,256,128]{2,1,0:T(8,128)} %fusion.2), calls=%async_computation.1 | async-start | bytes 4194304 | tf_op jit(solution)/shard_map/all_to_all | solution.py:22
  56.7 27.1 %all-to-all-done.1 = f32[16,256,128]{2,1,0:T(8,128)S(1)} async-done(((f32[16,256,128]{2,1,0:T(8,128)}), f32[16,256,128]{2,1,0:T(8,128)S(1)}, u32[]{:S(2)}, u32[]{:S(2)}) %all-to-all-start.1) | async-done | bytes 2097184 | tf_op jit(solution)/shard_map/all_to_all | solution.py:22
  83.8 0.1 reduce_sum.45
  83.9 0.0 copy-done
  83.9 0.1 add_tanh_fusion.2
  84.0 0.1 broadcast_in_dim.7
  84.1 23.4 %all_to_all.39 = f32[8,256,128]{2,1,0:T(8,128)S(1)} all-to-all(f32[8,256,128]{2,1,0:T(8,128)S(1)} %broadcast_in_dim.7), channel_id=1, replica_groups=mesh['row'=8,'col'=16] {'row'}, dimensions={0} | all-to-all | bytes 2097152 | tf_op jit(solution)/shard_map/all_to_all | solution.py:34
  107.5 11.6 %fusion.3 = f32[16,256,128]{2,1,0:T(8,128)S(1)} fusion(bf16[16,256,2048]{2,1,0:T(8,128)(2,1)} %bitcast.25, f32[2048,128,1]{1,0,2:T(8,128)S(1)} %bitcast.30), kind=kOutput, calls=%fused_computation.9 | convolution fusion | flops 6442450944 | bytes 19922944 | tf_op jit(solution)/shard_map/dot_general | solution.py:63
  119.1 31.3 %all_to_all.40 = f32[16,256,128]{2,1,0:T(8,128)S(1)} all-to-all(f32[16,256,128]{2,1,0:T(8,128)S(1)} %fusion.3), channel_id=1, replica_groups=mesh['row'=8,'col'=16] {'col'}, dimensions={0} | all-to-all | bytes 4194304 | tf_op jit(solution)/shard_map/all_to_all | solution.py:22
  150.4 0.1 reduce_sum.48
  150.5 0.1 add_tanh_fusion.1
  150.6 0.1 broadcast_in_dim.8
  150.7 18.6 %all_to_all.41 = f32[8,256,128]{2,1,0:T(8,128)S(1)} all-to-all(f32[8,256,128]{2,1,0:T(8,128)S(1)} %broadcast_in_dim.8), channel_id=1, replica_groups=mesh['row'=8,'col'=16] {'row'}, dimensions={0} | all-to-all | bytes 2097152 | tf_op jit(solution)/shard_map/all_to_all | solution.py:34
  169.3 11.6 %fusion.4 = f32[16,256,128]{2,1,0:T(8,128)S(1)} fusion(bf16[16,256,2048]{2,1,0:T(8,128)(2,1)} %bitcast.26, f32[2048,128,1]{1,0,2:T(8,128)S(1)} %bitcast.29), kind=kOutput, calls=%fused_computation.10 | convolution fusion | flops 6442450944 | bytes 19922944 | tf_op jit(solution)/shard_map/dot_general | solution.py:63
  180.9 31.7 %all_to_all.42 = f32[16,256,128]{2,1,0:T(8,128)S(1)} all-to-all(f32[16,256,128]{2,1,0:T(8,128)S(1)} %fusion.4), channel_id=1, replica_groups=mesh['row'=8,'col'=16] {'col'}, dimensions={0} | all-to-all | bytes 4194304 | tf_op jit(solution)/shard_map/all_to_all | solution.py:22
  212.6 0.1 reduce_sum.49
  212.7 0.8 add_tanh_fusion
  (2 shorter events, 0.0 us)
Async XLA Ops:
  2.0 29.0 %all-to-all-start = ((f32[8,256,128]{2,1,0:T(8,128)}), f32[8,256,128]{2,1,0:T(8,128)S(1)}, u32[]{:S(2)}, u32[]{:S(2)}) async-start(f32[8,256,128]{2,1,0:T(8,128)} %broadcast_in_dim.6), calls=%async_computation | async-start | bytes 2097152 | tf_op jit(solution)/shard_map/all_to_all | solution.py:34
  31.0 19.9 %all-to-all-start.2 = ((f32[16,1,256]{2,1,0:T(1,128)}), f32[16,1,256]{2,1,0:T(1,128)S(1)}, u32[]{:S(2)}, u32[]{:S(2)}) async-start(f32[16,1,256]{2,1,0:T(1,128)} %bitcast.3), calls=%async_computation.2 | async-start | bytes 32768 | tf_op jit(solution)/shard_map/all_to_all | solution.py:22
  37.4 46.5 %copy-start = (f32[256,128]{1,0:T(8,128)S(1)}, f32[256,128]{1,0:T(8,128)}, u32[]{:S(2)}) copy-start(f32[256,128]{1,0:T(8,128)} %param.4) | copy-start | bytes 393220
  50.9 32.8 %all-to-all-start.1 = ((f32[16,256,128]{2,1,0:T(8,128)}), f32[16,256,128]{2,1,0:T(8,128)S(1)}, u32[]{:S(2)}, u32[]{:S(2)}) async-start(f32[16,256,128]{2,1,0:T(8,128)} %fusion.2), calls=%async_computation.1 | async-start | bytes 4194304 | tf_op jit(solution)/shard_map/all_to_all | solution.py:22
where the time goes:
time: 214 us; the launch traced here: 213 us
  blocking collectives  105 us (49%)
  matrix products  36.7 us (17%)
  waiting for transfers between devices  27.1 us (13%)
  other arithmetic  20 us (9%)
  starting transfers between devices  19.6 us (9%)
  local copies, waits for them, and re-layouts  4.99 us (2%)
    all_to_all x2, blocking collectives, sum_at_owner(): lax.all_to_all(parts, axis, split_axis=0, concat_axis=0, tiled=True)  63 us
    all_to_all x2, blocking collectives, copy_for_each(): lax.all_to_all(jnp.broadcast_to(array[None], (count, *array.shape)), axis...  42 us
    dot_general x3, matrix products, shards(): jnp.dot(adjacency, collect(current, 'row', 0), precision=lax.Precision.HI...  36.7 us
    all_to_all x2, waiting for transfers between devices, sum_at_owner(): lax.all_to_all(parts, axis, split_axis=0, concat_axis=0, tiled=True)  27.1 us
    reduce_sum x1, other arithmetic, shards(): energy = sum_at_owner(jnp.sum(wide_tile * wide_tile, axis=1), 'col', 0)  17.9 us
    all_to_all x2, starting transfers between devices, sum_at_owner(): lax.all_to_all(parts, axis, split_axis=0, concat_axis=0, tiled=True)  12.1 us
    all_to_all x1, starting transfers between devices, copy_for_each(): lax.all_to_all(jnp.broadcast_to(array[None], (count, *array.shape)), axis...  7.48 us
  transfers between devices with their start and end apart: 3, of which 1 were waited for; matrix products, arithmetic and copies ran while one was open for 16% of the time, Pallas kernels for 0%

commit v1 on v0

v1 whole, which is shorter than its diff:
```python
import jax
import jax.numpy as jnp
from jax import lax
from jax.experimental import pallas as pl
from jax.experimental.pallas import tpu as pltpu
from jax.sharding import PartitionSpec as P

STEPS = 3
EPSILON = 1e-05
RETAIN = 0.8
TELEPORT = 0.2
NODES = 32768
F32, BF16 = jnp.float32, jnp.bfloat16
MESH = pl.DeviceIdType.MESH
VMEM = pltpu.VMEM


def low_lanes(rows=128):
    return lax.broadcasted_iota(jnp.int32, (rows, 128), 1) < 64


def fold(top, bottom):
    low = low_lanes(top.shape[0])
    return jnp.where(low, top, bottom) + pltpu.roll(jnp.where(low, bottom, top), 64, 1)


def kernel(
    src_ref, val_ref, occ_ref, exp_ref, out_ref,
    a_ref, scale_ref, x_ref, rhs_ref, acc_ref, psrc_ref, inv_ref,
    core_out, core_in, col_out, col_in,
    e_part, e_core, e_out, e_in, last_ref,
    load_sem, ag_ss, ag_rs, core_ss, core_rs, col_ss, col_rs,
    ec_ss, ec_rs, e_ss, e_rs,
):
    row, col = lax.axis_index("row"), lax.axis_index("col")
    yh, x = row // 4, row % 4
    z, yl, core = col // 4, (col // 2) % 2, col % 2
    sibling = (row, z * 4 + yl * 2 + 1 - core)

    loads = []
    for c in range(16):
        place = (c % 2) * 8 + c // 2
        loads.append(
            pltpu.make_async_copy(
                val_ref.at[pl.ds(c * 256, 256)],
                a_ref.at[pl.ds(place * 256, 256)],
                load_sem.at[c],
            )
        )
        loads[-1].start()

    row_mates = []
    for dy in (0, 1):
        for dx in (1, 3, 2, 0):
            if dx or dy:
                row_mates.append((((yh + dy) % 2) * 4 + (x + dx) % 4, col))
    col_mates = []
    for dz in (2, 1, 3, 0):
        for dy in (1, 0):
            if dz or dy:
                zz, yy = (z + dz) % 4, (yl + dy) % 2
                col_mates.append((zz * 2 + yy, (row, zz * 4 + yy * 2 + core)))

    barrier = pltpu.get_barrier_semaphore()
    mates = row_mates + [m for _, m in col_mates] + [sibling]
    for mate in mates:
        pl.semaphore_signal(barrier, inc=1, device_id=mate, device_id_type=MESH)

    low = low_lanes()
    top, bottom = src_ref[0:128], src_ref[128:256]
    packed = (
        jnp.where(low, top, pltpu.roll(bottom, 64, 1)),
        jnp.where(low, pltpu.roll(top, 64, 1), bottom),
    )
    for h in range(2):
        psrc_ref[h] = packed[h]
        x_ref[0, h, row] = packed[h]
    pl.semaphore_wait(barrier, len(mates))

    def spread(s, h):
        copies = []
        for i, mate in enumerate(row_mates):
            copies.append(
                pltpu.make_async_remote_copy(
                    x_ref.at[s, h, row], x_ref.at[s, h, row],
                    ag_ss.at[s, h, mate[0]], ag_rs.at[s, h, row],
                    device_id=mate, device_id_type=MESH,
                )
            )
        return copies

    def arrival(s, h, a):
        return pltpu.make_async_remote_copy(
            x_ref.at[s, h, a], x_ref.at[s, h, a],
            ag_ss.at[s, h, a], ag_rs.at[s, h, a],
            device_id=(a, col), device_id_type=MESH,
        )

    def to_sibling(s, h, zz):
        return pltpu.make_async_remote_copy(
            core_out.at[s, h, zz], core_in.at[s, h, zz],
            core_ss.at[s, h, zz], core_rs.at[s, h, zz],
            device_id=sibling, device_id_type=MESH,
        )

    def to_owner(s, h, zz, yy):
        return pltpu.make_async_remote_copy(
            col_out.at[s, h, zz * 2 + yy], col_in.at[s, h, z * 2 + yl],
            col_ss.at[s, h, zz * 2 + yy], col_rs.at[s, h, z * 2 + yl],
            device_id=(row, zz * 4 + yy * 2 + core), device_id_type=MESH,
        )

    def from_mate(s, h, slot, mate):
        return pltpu.make_async_remote_copy(
            col_out.at[s, h, slot], col_in.at[s, h, slot],
            col_ss.at[s, h, slot], col_rs.at[s, h, slot],
            device_id=mate, device_id_type=MESH,
        )

    for h in range(2):
        for copy in spread(0, h):
            copy.start()

    occ = occ_ref[...].astype(F32)
    scale = occ * ((jnp.int32(1) << (exp_ref[...] + 3)).astype(F32) * 0.125)
    for j in range(16):
        scale_ref[:, j * 128 : (j + 1) * 128] = jnp.broadcast_to(scale[:, j : j + 1], (32, 128))
    ones = jnp.ones((8, 128), F32)
    for c in range(16):
        loads[c].wait()
        place = (c % 2) * 8 + c // 2

        for half in range(2):
            def tile(i, _, place=place, half=half, c=c):
                base = pl.multiple_of(place * 256 + half * 128 + i * 16, 16)
                total = jnp.zeros((16, 128), F32)
                for j in range(16):
                    lanes = slice(j * 128, (j + 1) * 128)
                    part = a_ref[pl.ds(base, 16), lanes].astype(F32)
                    part = part * scale_ref[c * 2 + half : c * 2 + half + 1, lanes]
                    total += part * part
                    a_ref[pl.ds(base, 16), lanes] = part.astype(BF16)
                acc_ref[pl.ds(half * 128 + i * 16, 16), :] = total
                return 0

            lax.fori_loop(0, 8, tile, 0, unroll=2)
        e_part[c % 2, c // 2] = lax.dot_general(
            ones, acc_ref[0:256, :], (((1,), (1,)), ((), ())),
            precision=lax.Precision.HIGHEST, preferred_element_type=F32,
        )
    e_sib = pltpu.make_async_remote_copy(
        e_part.at[1 - core], e_core, ec_ss, ec_rs, device_id=sibling, device_id_type=MESH
    )
    e_sib.start()
    e_sib.wait()
    e_out[...] = e_part[core] + e_core[...]
    e_copies = []
    for slot, mate in col_mates:
        copy = pltpu.make_async_remote_copy(
            e_out.at[slot], e_in.at[z * 2 + yl], e_ss.at[slot], e_rs.at[z * 2 + yl],
            device_id=mate, device_id_type=MESH,
        )
        copy.start()
        e_copies.append(copy)

    def load_rhs(s, h, a):
        part = x_ref[s, h, a]
        high = part.astype(BF16).astype(F32)
        rest = pltpu.roll(part - high, 64, 1)
        base = pl.multiple_of(a * 256, 256)
        rhs_ref[pl.ds(base, 128), :] = jnp.where(low, high, rest).astype(BF16)
        rhs_ref[pl.ds(base + 128, 128), :] = jnp.where(low, rest, high).astype(BF16)

    near = pl.multiple_of(yh * 1024, 1024)
    far = pl.multiple_of((1 - yh) * 1024, 1024)

    def multiply(s, h):
        load_rhs(s, h, row)
        for dx in (1, 3, 2):
            a = yh * 4 + (x + dx) % 4
            arrival(s, h, a).wait_recv()
            load_rhs(s, h, a)

        def first(m, _):
            rows = pl.ds(pl.multiple_of(m * 512, 512), 512)
            acc_ref[rows, :] = jnp.dot(
                a_ref[rows, pl.ds(near, 1024)], rhs_ref[pl.ds(near, 1024), :],
                preferred_element_type=F32,
            )
            return 0

        lax.fori_loop(0, 8, first, 0)
        for dx in (1, 3, 2, 0):
            a = (1 - yh) * 4 + (x + dx) % 4
            arrival(s, h, a).wait_recv()
            load_rhs(s, h, a)

        def second(whose, zz):
            rows = pl.ds(pl.multiple_of(whose * 2048 + zz * 512, 512), 512)
            total = acc_ref[rows, :] + jnp.dot(
                a_ref[rows, pl.ds(far, 1024)], rhs_ref[pl.ds(far, 1024), :],
                preferred_element_type=F32,
            )
            return [fold(total[y * 256 : y * 256 + 128], total[y * 256 + 128 : y * 256 + 256]) for y in (0, 1)]

        def theirs(it, _):
            zz = (z + 1 + it) % 4
            blocks = second(1 - core, zz)
            for y in (0, 1):
                core_out[s, h, zz, y] = blocks[y]
            to_sibling(s, h, zz).start()
            return 0

        lax.fori_loop(0, 4, theirs, 0)

        def mine(it, _):
            zz = (z + 1 + it) % 4
            blocks = second(core, zz)
            to_sibling(s, h, zz).wait_recv()
            for y in (0, 1):
                col_out[s, h, zz * 2 + y] = blocks[y] + core_in[s, h, zz, y]

            @pl.when(it != 3)
            def _():
                for dy in (1, 0):
                    to_owner(s, h, zz, (yl + dy) % 2).start()

            @pl.when(it == 3)
            def _():
                to_owner(s, h, z, 1 - yl).start()

            return 0

        lax.fori_loop(0, 4, mine, 0)

    def finish(s, h):
        total = col_out[s, h, z * 2 + yl]
        for slot, mate in col_mates:
            from_mate(s, h, slot, mate).wait_recv()
            total = total + col_in[s, h, slot]
        new = jnp.tanh(RETAIN * total * inv_ref[...] + TELEPORT * psrc_ref[h])
        if s < STEPS - 1:
            x_ref[s + 1, h, row] = new
            for copy in spread(s + 1, h):
                copy.start()
        else:
            last_ref[h] = new

    for s in range(STEPS):
        for h in range(2):
            multiply(s, h)
        if s == 0:
            energy = e_out[z * 2 + yl]
            for slot, mate in col_mates:
                pltpu.make_async_remote_copy(
                    e_out.at[slot], e_in.at[slot], e_ss.at[slot], e_rs.at[slot],
                    device_id=mate, device_id_type=MESH,
                ).wait_recv()
                energy = energy + e_in[slot]
            across = [
                jnp.transpose(jnp.broadcast_to(energy[0:1, k * 128 : (k + 1) * 128], (128, 128)))
                for k in range(2)
            ]
            mean = jnp.where(low, across[0], across[1]) / NODES
            inv_ref[...] = 1.0 / (jnp.sqrt(NODES * 1.0) * jnp.sqrt(mean + EPSILON))
        for h in range(2):
            finish(s, h)

    left, right = last_ref[0], last_ref[1]
    out_ref[0:128] = jnp.where(low, left, pltpu.roll(right, 64, 1))
    out_ref[128:256] = jnp.where(low, pltpu.roll(left, 64, 1), right)

    for copy in e_copies:
        copy.wait_send()
    for s in range(STEPS):
        for h in range(2):
            for copy in spread(s, h):
                copy.wait_send()
            for zz in range(4):
                to_sibling(s, h, zz).wait_send()
            for slot, mate in col_mates:
                from_mate(s, h, slot, mate).wait_send()


def shards(source, value, occupancy, exponent):
    vmem = pl.BlockSpec(memory_space=VMEM)
    dma = pltpu.SemaphoreType.DMA
    halves = (STEPS, 2)
    return pl.pallas_call(
        kernel,
        out_shape=jax.ShapeDtypeStruct((256, 128), F32),
        in_specs=[vmem, pl.BlockSpec(memory_space=pl.ANY), vmem, vmem],
        out_specs=vmem,
        scratch_shapes=[
            VMEM((4096, 2048), BF16),
            VMEM((32, 2048), F32),
            VMEM((*halves, 8, 128, 128), F32),
            VMEM((2048, 128), BF16),
            VMEM((4096, 128), F32),
            VMEM((2, 128, 128), F32),
            VMEM((128, 128), F32),
            VMEM((*halves, 4, 2, 128, 128), F32),
            VMEM((*halves, 4, 2, 128, 128), F32),
            VMEM((*halves, 8, 128, 128), F32),
            VMEM((*halves, 8, 128, 128), F32),
            VMEM((2, 8, 8, 256), F32),
            VMEM((8, 8, 256), F32),
            VMEM((8, 8, 256), F32),
            VMEM((8, 8, 256), F32),
            VMEM((2, 128, 128), F32),
            dma((16,)),
            dma((*halves, 8)), dma((*halves, 8)),
            dma((*halves, 4)), dma((*halves, 4)),
            dma((*halves, 8)), dma((*halves, 8)),
            dma, dma,
            dma((8,)), dma((8,)),
        ],
        compiler_params=pltpu.CompilerParams(
            collective_id=0, has_side_effects=True, vmem_limit_bytes=58 * 2**20
        ),
        cost_estimate=pl.CostEstimate(
            flops=3 * 2 * 4096 * 2048 * 256, bytes_accessed=17 * 2**20, transcendentals=3 * 32768
        ),
    )(source, value, occupancy, exponent)


def solution(mesh):
    placed = (P(("row", "col"), None), P("row", "col"), P("row", "col"), P("row", "col"))
    return jax.shard_map(
        shards, mesh=mesh, in_specs=placed, out_specs=P(("row", "col"), None), check_vma=False
    )
```

time: 214 us -> 108 us (0.50)
  blocking collectives: 105 us -> 0 us
  Pallas kernels: 0 us -> 104 us
  matrix products: 36.7 us -> 0 us
  waiting for transfers between devices: 27.1 us -> 0 us
  other arithmetic: 20 us -> 0 us
  starting transfers between devices: 19.6 us -> 0 us
    all_to_all x4 -> x0, blocking collectives: 105 us -> none  [the longest x2 63 us: sum_at_owner(): lax.all_to_all(parts, axis, split_axis=0, concat_axis=0, tiled=True)]
    pallas_call x0 -> x1, Pallas kernels: none -> 104 us  [shards(): pl.pallas_call(kernel, out_shape=jax.ShapeDtypeStruct((256, 128), F32), i...]
    dot_general x3 -> x0, matrix products: 36.7 us -> none  [shards(): jnp.dot(adjacency, collect(current, 'row', 0), precision=lax.Precision.HI...]
    all_to_all x3 -> x0, waiting for transfers between devices: 27.1 us -> none  [the longest x2 27.1 us: sum_at_owner(): lax.all_to_all(parts, axis, split_axis=0, concat_axis=0, tiled=True)]
    all_to_all x3 -> x0, starting transfers between devices: 19.6 us -> none  [the longest x2 12.1 us: sum_at_owner(): lax.all_to_all(parts, axis, split_axis=0, concat_axis=0, tiled=True)]
    reduce_sum x5 -> x0, other arithmetic: 18.3 us -> none  [the longest x1 17.9 us: shards(): energy = sum_at_owner(jnp.sum(wide_tile * wide_tile, axis=1), 'col', 0)]
    unnamed x2 -> x3, local copies, waits for them, and re-layouts: 0.01 us -> 4.31 us
    mul x2 -> x0, local copies, waits for them, and re-layouts: 2.88 us -> none  [the longest x1 2.81 us: expand_tile(): value.astype(jnp.float32)]
  transfers between devices with their start and end apart: 3 -> 0, of which waited for: 1 -> 0; matrix products, arithmetic and copies ran while one was open for 16% -> 0% of each run, Pallas kernels for 0% -> 0%
where the time goes in v1:
time: 108 us
  Pallas kernels  104 us (96%)
  local copies, waits for them, and re-layouts  4.31 us (4%)
    pallas_call x1, Pallas kernels, shards(): pl.pallas_call(kernel, out_shape=jax.ShapeDtypeStruct((256, 128), F32), i...  104 us
    unnamed x3, local copies, waits for them, and re-layouts  4.31 us

profile of v1, /device:TPU:1, one launch (start us, length us, event | category | flops | bytes accessed | tf_op | source)
XLA Modules:
  0.0 108.1 jit_solution(2945073287054335433)
XLA Ops:
  0.0 1.4 %copy.5.occ_ref = s32[32,16]{1,0:T(8,128)} copy(s32[32,16]{0,1:T(8,128)} %param.6) | data formatting | bytes 4096 | tf_op args[2]
  1.4 1.4 %copy.6.exp_ref = s32[32,16]{1,0:T(8,128)} copy(s32[32,16]{0,1:T(8,128)} %param.7) | data formatting | bytes 4096 | tf_op args[3]
  2.7 103.8 %shard_map.46 = f32[256,128]{1,0:T(8,128)} custom-call(f32[256,128]{1,0:T(8,128)} %src_ref.1, bf16[4096,2048]{1,0:T(8,128)(2,1)} %val_ref.1, s32[32,16]{1,0:T(8,128)} %copy.5.occ_ref, s32[32,16]{1,0:T(8,128)} %copy.6.exp_ref), custom_call_target="tpu_custom_call" | custom-call | flops 12884901888 | bytes 17825792 | tf_op jit(solution)/shard_map/pallas_call | solution.py:289
  106.5 1.6 %copy.8 = f32[256,128]{1,0:T(8,128)} copy(f32[256,128]{1,0:T(8,128)} %shard_map.46) | data formatting | bytes 262144

commit v2 on v1

v2 whole, which is shorter than its diff:
```python
import jax
import jax.numpy as jnp
from jax import lax
from jax.experimental import pallas as pl
from jax.experimental.pallas import tpu as pltpu
from jax.sharding import PartitionSpec as P

STEPS = 3
EPSILON = 1e-05
RETAIN = 0.8
TELEPORT = 0.2
NODES = 32768
FORWARDED = (1, 3, 2)
AHEAD = 6
F32, BF16 = jnp.float32, jnp.bfloat16
MESH = pl.DeviceIdType.MESH
VMEM = pltpu.VMEM


def low_lanes(rows=128):
    return lax.broadcasted_iota(jnp.int32, (rows, 128), 1) < 64


def fold(top, bottom):
    low = low_lanes(top.shape[0])
    return jnp.where(low, top, bottom) + pltpu.roll(jnp.where(low, bottom, top), 64, 1)


def kernel(
    src_hbm, val_ref, occ_hbm, exp_hbm, out_ref,
    src_ref, occ_ref, exp_ref, small_sem,
    stage_ref, a_ref, scale_ref, x_ref, rhs_ref, acc_ref, psrc_ref, inv_ref,
    core_out, core_in, col_out, col_in,
    squares, tall, e_part, e_core, e_out, e_in, last_ref,
    load_sem, ag_ss, ag_rs, core_ss, core_rs, col_ss, col_rs,
    ec_ss, ec_rs, e_ss, e_rs,
):
    row, col = lax.axis_index("row"), lax.axis_index("col")
    yh, x = row // 4, row % 4
    z, yl, core = col // 4, (col // 2) % 2, col % 2
    sibling = (row, z * 4 + yl * 2 + 1 - core)

    def load(place):
        owner = place % 8 * 2 + place // 8
        return pltpu.make_async_copy(
            val_ref.at[pl.ds(pl.multiple_of(owner * 256, 256), 256)],
            stage_ref.at[place % AHEAD],
            load_sem.at[place],
        )

    small = [
        pltpu.make_async_copy(there, here, small_sem.at[k])
        for k, (there, here) in enumerate(
            [(src_hbm, src_ref), (occ_hbm, occ_ref), (exp_hbm, exp_ref)]
        )
    ]
    for copy in small:
        copy.start()

    row_mates = []
    for dy in (0, 1):
        for dx in (1, 3, 2, 0):
            if dx or dy:
                row_mates.append((((yh + dy) % 2) * 4 + (x + dx) % 4, col))
    col_mates = []
    for dz in (2, 1, 3, 0):
        for dy in (1, 0):
            if dz or dy:
                zz, yy = (z + dz) % 4, (yl + dy) % 2
                col_mates.append((zz * 2 + yy, (row, zz * 4 + yy * 2 + core)))

    barrier = pltpu.get_barrier_semaphore()
    mates = row_mates + [m for _, m in col_mates] + [sibling]
    for mate in mates:
        pl.semaphore_signal(barrier, inc=1, device_id=mate, device_id_type=MESH)

    for place in range(AHEAD):
        load(place).start()
    low = low_lanes()
    small[0].wait()
    top, bottom = src_ref[0:128], src_ref[128:256]
    packed = (
        jnp.where(low, top, pltpu.roll(bottom, 64, 1)),
        jnp.where(low, pltpu.roll(top, 64, 1), bottom),
    )
    for h in range(2):
        psrc_ref[h] = packed[h]
        x_ref[0, h, row] = packed[h]
    pl.semaphore_wait(barrier, len(mates))

    partner = (1 - yh) * 4 + x

    def spread(s, h):
        mates = [partner] + [yh * 4 + (x + dx) % 4 for dx in (1, 3, 2)]
        mates += [(1 - yh) * 4 + (x + dx) % 4 for dx in (2, 1, 3) if s == 0 or dx not in FORWARDED]
        return [
            pltpu.make_async_remote_copy(
                x_ref.at[s, h, row], x_ref.at[s, h, row],
                ag_ss.at[s, h, mate], ag_rs.at[s, h, row],
                device_id=(mate, col), device_id_type=MESH,
            )
            for mate in mates
        ]

    def forward(s, h):
        if s == 0:
            return []
        return [
            pltpu.make_async_remote_copy(
                x_ref.at[s, h, partner], x_ref.at[s, h, partner],
                ag_ss.at[s, h, 8 + dx], ag_rs.at[s, h, partner],
                device_id=(yh * 4 + (x + dx) % 4, col), device_id_type=MESH,
            )
            for dx in FORWARDED
        ]

    def pass_on(s, h):
        arrival(s, h, partner).wait_recv()
        for copy in forward(s, h):
            copy.start()

    def arrival(s, h, a):
        return pltpu.make_async_remote_copy(
            x_ref.at[s, h, a], x_ref.at[s, h, a],
            ag_ss.at[s, h, a], ag_rs.at[s, h, a],
            device_id=(a, col), device_id_type=MESH,
        )

    def to_sibling(s, h, pair):
        return pltpu.make_async_remote_copy(
            core_out.at[s, h, pair], core_in.at[s, h, pair],
            core_ss.at[s, h, pair], core_rs.at[s, h, pair],
            device_id=sibling, device_id_type=MESH,
        )

    def to_owner(s, h, zz, yy):
        return pltpu.make_async_remote_copy(
            col_out.at[s, h, zz * 2 + yy], col_in.at[s, h, z * 2 + yl],
            col_ss.at[s, h, zz * 2 + yy], col_rs.at[s, h, z * 2 + yl],
            device_id=(row, zz * 4 + yy * 2 + core), device_id_type=MESH,
        )

    def from_mate(s, h, slot, mate):
        return pltpu.make_async_remote_copy(
            col_out.at[s, h, slot], col_in.at[s, h, slot],
            col_ss.at[s, h, slot], col_rs.at[s, h, slot],
            device_id=mate, device_id_type=MESH,
        )

    for copy in spread(0, 0):
        copy.start()

    small[1].wait()
    small[2].wait()
    tall[...] = jnp.zeros_like(tall)
    tall[0:16, 0:32] = occ_ref[...].astype(F32) * (
        (jnp.int32(1) << (exp_ref[...] + 3)).astype(F32) * 0.125
    )
    scale = jnp.transpose(tall[...])
    for j in range(16):
        across = jnp.broadcast_to(scale[0:32, j : j + 1], (32, 128))
        for i in range(32):
            scale_ref[i, :, j * 128 : (j + 1) * 128] = jnp.broadcast_to(
                across[i : i + 1], (16, 128)
            ).astype(BF16)

    squares[0:256, :] = jnp.zeros((256, 128), F32)

    def sum_lanes(place):
        ones = jnp.ones((8, 128), BF16)
        dims = (((1,), (1,)), ((), ()))
        part = squares[pl.ds(pl.multiple_of(place * 256, 256), 256), :]
        high = part.astype(BF16)
        rest = (part - high.astype(F32)).astype(BF16)
        e_part[place // 8, place % 8] = lax.dot_general(
            ones, high, dims, preferred_element_type=F32
        ) + lax.dot_general(ones, rest, dims, preferred_element_type=F32)

    def base_of(a):
        return ((a // 4 + yh) % 2 * 4 + (a % 4 + 4 - x) % 4) * 256

    bases = [base_of(a) for a in range(8)]

    def scale_rows(place, _):
        load(place).wait()
        owner = place % 8 * 2 + place // 8
        slot = place % AHEAD
        sum_lanes(jnp.maximum(place - 1, 0))
        for half in range(2):
            base = pl.multiple_of(place * 256 + half * 128, 128)
            for q in range(4):
                total = [jnp.zeros((16, 128), F32)] * 2
                rows = [pl.ds(half * 128 + q * 32 + r * 16, 16) for r in range(2)]
                out_rows = [pl.ds(base + q * 32 + r * 16, 16) for r in range(2)]
                for j in range(16):
                    lanes = slice(j * 128, (j + 1) * 128)
                    out_lanes = pl.ds(pl.multiple_of(bases[j // 2] + j % 2 * 128, 128), 128)
                    factor = scale_ref[owner * 2 + half, :, lanes]
                    for r in range(2):
                        part = stage_ref[slot, rows[r], lanes] * factor
                        a_ref[out_rows[r], out_lanes] = part
                        wide = part.astype(F32)
                        total[r] = total[r] + wide * wide
                for r in range(2):
                    squares[out_rows[r], :] = total[r]

        @pl.when(place < 16 - AHEAD)
        def _():
            load(place + AHEAD).start()

        return 0

    lax.fori_loop(0, 16, scale_rows, 0)
    sum_lanes(15)
    for copy in spread(0, 1):
        copy.start()

    e_sib = pltpu.make_async_remote_copy(
        e_part.at[1 - core], e_core, ec_ss, ec_rs, device_id=sibling, device_id_type=MESH
    )

    def e_mate(slot, mate, there):
        return pltpu.make_async_remote_copy(
            e_out.at[slot], e_in.at[there], e_ss.at[slot], e_rs.at[there],
            device_id=mate, device_id_type=MESH,
        )

    def send_energy():
        e_sib.wait()
        e_out[...] = e_part[core] + e_core[...]
        for slot, mate in col_mates:
            e_mate(slot, mate, z * 2 + yl).start()

    def take_energy():
        energy = e_out[z * 2 + yl]
        for slot, mate in col_mates:
            e_mate(slot, mate, slot).wait_recv()
            energy = energy + e_in[slot]
        across = [
            jnp.transpose(jnp.broadcast_to(energy[0:1, k * 128 : (k + 1) * 128], (128, 128)))
            for k in range(2)
        ]
        mean = jnp.where(low, across[0], across[1]) / NODES
        inv_ref[...] = 1.0 / (jnp.sqrt(NODES * 1.0) * jnp.sqrt(mean + EPSILON))

    def load_rhs(s, h, a):
        part = x_ref[s, h, a]
        high = part.astype(BF16).astype(F32)
        rest = pltpu.roll(part - high, 64, 1)
        base = pl.multiple_of(base_of(a), 256)
        rhs_ref[pl.ds(base, 128), :] = jnp.where(low, high, rest).astype(BF16)
        rhs_ref[pl.ds(base + 128, 128), :] = jnp.where(low, rest, high).astype(BF16)

    def multiply_near(s, h):
        load_rhs(s, h, row)
        load_rhs(s, h, partner)
        for dx in (1, 3, 2):
            a = yh * 4 + (x + dx) % 4
            arrival(s, h, a).wait_recv()
            load_rhs(s, h, a)

        def tile(m, _):
            rows = pl.ds(pl.multiple_of(m * 1024, 1024), 1024)
            acc_ref[rows, :] = jnp.dot(
                a_ref[rows, 0:1280], rhs_ref[0:1280, :],
                preferred_element_type=F32,
            )
            return 0

        lax.fori_loop(0, 4, tile, 0)

    def far_tile(whose, pair):
        rows = pl.ds(pl.multiple_of(whose * 2048 + pair * 1024, 1024), 1024)
        total = acc_ref[rows, :] + jnp.dot(
            a_ref[rows, 1280:2048], rhs_ref[1280:2048, :],
            preferred_element_type=F32,
        )
        return [fold(total[b * 256 : b * 256 + 128], total[b * 256 + 128 : b * 256 + 256]) for b in range(4)]

    def multiply_far(s, h):
        for dx in (1, 3, 2):
            a = (1 - yh) * 4 + (x + dx) % 4
            arrival(s, h, a).wait_recv()
            load_rhs(s, h, a)

        def theirs(it, _):
            pair = (z // 2 + 1 + it) % 2
            blocks = far_tile(1 - core, pair)
            for b in range(4):
                core_out[s, h, pair, b] = blocks[b]
            to_sibling(s, h, pair).start()
            return 0

        lax.fori_loop(0, 2, theirs, 0)

    def join(s, h):
        def mine(it, _):
            pair = (z // 2 + 1 + it) % 2
            blocks = far_tile(core, pair)
            to_sibling(s, h, pair).wait_recv()
            for b in range(4):
                col_out[s, h, pair * 4 + b] = blocks[b] + core_in[s, h, pair, b]
            for dz in (1, 0):
                zz = pair * 2 + (z + dz) % 2
                for dy in (1, 0):
                    if dz or dy:
                        to_owner(s, h, zz, (yl + dy) % 2).start()
                    else:

                        @pl.when(it == 0)
                        def _():
                            to_owner(s, h, zz, yl).start()

            return 0

        lax.fori_loop(0, 2, mine, 0)

    def finish(s, h):
        total = col_out[s, h, z * 2 + yl]
        for slot, mate in col_mates:
            from_mate(s, h, slot, mate).wait_recv()
            total = total + col_in[s, h, slot]
        new = jnp.tanh(RETAIN * total * inv_ref[...] + TELEPORT * psrc_ref[h])
        if s < STEPS - 1:
            x_ref[s + 1, h, row] = new
            for copy in spread(s + 1, h):
                copy.start()
        else:
            last_ref[h] = new

    pass_on(0, 0)
    e_sib.start()
    multiply_near(0, 0)
    multiply_far(0, 0)
    send_energy()
    join(0, 0)
    for s in range(STEPS):
        pass_on(s, 1)
        multiply_near(s, 1)
        if s == 0:
            take_energy()
        multiply_far(s, 1)
        if s < STEPS - 1:
            finish(s, 0)
            join(s, 1)
            pass_on(s + 1, 0)
            multiply_near(s + 1, 0)
            multiply_far(s + 1, 0)
            finish(s, 1)
            join(s + 1, 0)
        else:
            join(s, 1)
            finish(s, 0)
            finish(s, 1)

    left, right = last_ref[0], last_ref[1]
    out_ref[0:128] = jnp.where(low, left, pltpu.roll(right, 64, 1))
    out_ref[128:256] = jnp.where(low, pltpu.roll(left, 64, 1), right)

    for slot, mate in col_mates:
        e_mate(slot, mate, slot).wait_send()
    for s in range(STEPS):
        for h in range(2):
            for copy in spread(s, h) + forward(s, h):
                copy.wait_send()
            for pair in range(2):
                to_sibling(s, h, pair).wait_send()
            for slot, mate in col_mates:
                from_mate(s, h, slot, mate).wait_send()


def shards(source, value, occupancy, exponent):
    vmem = pl.BlockSpec(memory_space=VMEM)
    dma = pltpu.SemaphoreType.DMA
    halves = (STEPS, 2)
    return pl.pallas_call(
        kernel,
        out_shape=jax.ShapeDtypeStruct((256, 128), F32),
        in_specs=[pl.BlockSpec(memory_space=pltpu.HBM)] * 4,
        out_specs=vmem,
        scratch_shapes=[
            VMEM((256, 128), F32),
            VMEM((16, 32), jnp.int32),
            VMEM((16, 32), jnp.int32),
            dma((3,)),
            VMEM((AHEAD, 256, 2048), BF16),
            VMEM((4096, 2048), BF16),
            VMEM((32, 16, 2048), BF16),
            VMEM((*halves, 8, 128, 128), F32),
            VMEM((2048, 128), BF16),
            VMEM((4096, 128), F32),
            VMEM((2, 128, 128), F32),
            VMEM((128, 128), F32),
            VMEM((*halves, 2, 4, 128, 128), F32),
            VMEM((*halves, 2, 4, 128, 128), F32),
            VMEM((*halves, 8, 128, 128), F32),
            VMEM((*halves, 8, 128, 128), F32),
            VMEM((4096, 128), F32),
            VMEM((128, 128), F32),
            VMEM((2, 8, 8, 256), F32),
            VMEM((8, 8, 256), F32),
            VMEM((8, 8, 256), F32),
            VMEM((8, 8, 256), F32),
            VMEM((2, 128, 128), F32),
            dma((16,)),
            dma((*halves, 12)), dma((*halves, 8)),
            dma((*halves, 2)), dma((*halves, 2)),
            dma((*halves, 8)), dma((*halves, 8)),
            dma, dma,
            dma((8,)), dma((8,)),
        ],
        compiler_params=pltpu.CompilerParams(
            collective_id=0, has_side_effects=True, vmem_limit_bytes=58 * 2**20
        ),
        cost_estimate=pl.CostEstimate(
            flops=3 * 2 * 4096 * 2048 * 256, bytes_accessed=17 * 2**20, transcendentals=3 * 32768
        ),
    )(source, value, occupancy.T, exponent.T)


def solution(mesh):
    placed = (P(("row", "col"), None), P("row", "col"), P("row", "col"), P("row", "col"))
    return jax.shard_map(
        shards, mesh=mesh, in_specs=placed, out_specs=P(("row", "col"), None), check_vma=False
    )
```

time: 108 us -> 87.9 us (0.81)
  Pallas kernels: 104 us -> 86.2 us
  local copies, waits for them, and re-layouts: 4.31 us -> 1.57 us
    pallas_call x1, Pallas kernels: 104 us -> 86.2 us  [shards(): pl.pallas_call(kernel, out_shape=jax.ShapeDtypeStruct((256, 128), F32), i...]
    unnamed x3 -> x1, local copies, waits for them, and re-layouts: 4.31 us -> 1.57 us
where the time goes in v2:
time: 87.9 us; the launch traced here: 87.8 us
  Pallas kernels  86.2 us (98%)
  local copies, waits for them, and re-layouts  1.57 us (2%)
    pallas_call x1, Pallas kernels, shards(): pl.pallas_call(kernel, out_shape=jax.ShapeDtypeStruct((256, 128), F32), i...  86.2 us

profile of v2, /device:TPU:1, one launch (start us, length us, event | category | flops | bytes accessed | tf_op | source)
XLA Modules:
  0.0 87.8 jit_solution(17818434219624572861)
XLA Ops:
  0.0 86.2 %shard_map.46 = f32[256,128]{1,0:T(8,128)} custom-call(f32[256,128]{1,0:T(8,128)} %src_hbm.1, bf16[4096,2048]{1,0:T(8,128)(2,1)} %val_ref.1, s32[16,32]{1,0:T(8,128)} %bitcast.2, s32[16,32]{1,0:T(8,128)} %bitcast.3), custom_call_target="tpu_custom_call" | custom-call | flops 12884901888 | bytes 17825792 | tf_op jit(solution)/shard_map/pallas_call | solution.py:376
  86.3 1.6 %copy.6 = f32[256,128]{1,0:T(8,128)} copy(f32[256,128]{1,0:T(8,128)} %shard_map.46) | data formatting | bytes 262144

commit v3 on v2

--- a/solution.py
+++ b/solution.py
@@ -12,6 +12,8 @@
 NODES = 32768
 FORWARDED = (1, 3, 2)
 AHEAD = 6
+CHUNKS = 2
+CHUNK = 128 // CHUNKS
 F32, BF16 = jnp.float32, jnp.bfloat16
 MESH = pl.DeviceIdType.MESH
 VMEM = pltpu.VMEM
@@ -90,41 +92,37 @@
 
     partner = (1 - yh) * 4 + x
 
-    def spread(s, h):
+    def rows_of(k):
+        return pl.ds(k * CHUNK, CHUNK)
+
+    def gather_copy(s, h, a, k, send, mate):
+        return pltpu.make_async_remote_copy(
+            x_ref.at[s, h, a, rows_of(k)], x_ref.at[s, h, a, rows_of(k)],
+            ag_ss.at[s, h, send, k], ag_rs.at[s, h, a, k],
+            device_id=(mate, col), device_id_type=MESH,
+        )
+
+    def spread(s, h, k):
         mates = [partner] + [yh * 4 + (x + dx) % 4 for dx in (1, 3, 2)]
         mates += [(1 - yh) * 4 + (x + dx) % 4 for dx in (2, 1, 3) if s == 0 or dx not in FORWARDED]
-        return [
-            pltpu.make_async_remote_copy(
-                x_ref.at[s, h, row], x_ref.at[s, h, row],
-                ag_ss.at[s, h, mate], ag_rs.at[s, h, row],
-                device_id=(mate, col), device_id_type=MESH,
-            )
-            for mate in mates
-        ]
-
-    def forward(s, h):
+        return [gather_copy(s, h, row, k, mate, mate) for mate in mates]
+
+    def forward(s, h, k):
         if s == 0:
             return []
         return [
-            pltpu.make_async_remote_copy(
-                x_ref.at[s, h, partner], x_ref.at[s, h, partner],
-                ag_ss.at[s, h, 8 + dx], ag_rs.at[s, h, partner],
-                device_id=(yh * 4 + (x + dx) % 4, col), device_id_type=MESH,
-            )
-            for dx in FORWARDED
+            gather_copy(s, h, partner, k, 8 + dx, yh * 4 + (x + dx) % 4) for dx in FORWARDED
         ]
 
+    def arrive(s, h, a):
+        for k in range(CHUNKS):
+            gather_copy(s, h, a, k, a, a).wait_recv()
+
     def pass_on(s, h):
-        arrival(s, h, partner).wait_recv()
-        for copy in forward(s, h):
-            copy.start()
-
-    def arrival(s, h, a):
-        return pltpu.make_async_remote_copy(
-            x_ref.at[s, h, a], x_ref.at[s, h, a],
-            ag_ss.at[s, h, a], ag_rs.at[s, h, a],
-            device_id=(a, col), device_id_type=MESH,
-        )
+        for k in range(CHUNKS):
+            gather_copy(s, h, partner, k, partner, partner).wait_recv()
+            for copy in forward(s, h, k):
+                copy.start()
 
     def to_sibling(s, h, pair):
         return pltpu.make_async_remote_copy(
@@ -133,22 +131,23 @@
             device_id=sibling, device_id_type=MESH,
         )
 
-    def to_owner(s, h, zz, yy):
+    def to_owner(s, h, zz, yy, k):
         return pltpu.make_async_remote_copy(
-            col_out.at[s, h, zz * 2 + yy], col_in.at[s, h, z * 2 + yl],
-            col_ss.at[s, h, zz * 2 + yy], col_rs.at[s, h, z * 2 + yl],
+            col_out.at[s, h, zz * 2 + yy, rows_of(k)], col_in.at[s, h, z * 2 + yl, rows_of(k)],
+            col_ss.at[s, h, zz * 2 + yy, k], col_rs.at[s, h, z * 2 + yl, k],
             device_id=(row, zz * 4 + yy * 2 + core), device_id_type=MESH,
         )
 
-    def from_mate(s, h, slot, mate):
+    def from_mate(s, h, slot, mate, k):
         return pltpu.make_async_remote_copy(
-            col_out.at[s, h, slot], col_in.at[s, h, slot],
-            col_ss.at[s, h, slot], col_rs.at[s, h, slot],
+            col_out.at[s, h, slot, rows_of(k)], col_in.at[s, h, slot, rows_of(k)],
+            col_ss.at[s, h, slot, k], col_rs.at[s, h, slot, k],
             device_id=mate, device_id_type=MESH,
         )
 
-    for copy in spread(0, 0):
-        copy.start()
+    for k in range(CHUNKS):
+        for copy in spread(0, 0, k):
+            copy.start()
 
     small[1].wait()
     small[2].wait()
@@ -212,8 +211,9 @@
 
     lax.fori_loop(0, 16, scale_rows, 0)
     sum_lanes(15)
-    for copy in spread(0, 1):
-        copy.start()
+    for k in range(CHUNKS):
+        for copy in spread(0, 1, k):
+            copy.start()
 
     e_sib = pltpu.make_async_remote_copy(
         e_part.at[1 - core], e_core, ec_ss, ec_rs, device_id=sibling, device_id_type=MESH
@@ -256,7 +256,7 @@
         load_rhs(s, h, partner)
         for dx in (1, 3, 2):
             a = yh * 4 + (x + dx) % 4
-            arrival(s, h, a).wait_recv()
+            arrive(s, h, a)
             load_rhs(s, h, a)
 
         def tile(m, _):
@@ -280,7 +280,7 @@
     def multiply_far(s, h):
         for dx in (1, 3, 2):
             a = (1 - yh) * 4 + (x + dx) % 4
-            arrival(s, h, a).wait_recv()
+            arrive(s, h, a)
             load_rhs(s, h, a)
 
         def theirs(it, _):
@@ -300,33 +300,36 @@
             to_sibling(s, h, pair).wait_recv()
             for b in range(4):
                 col_out[s, h, pair * 4 + b] = blocks[b] + core_in[s, h, pair, b]
-            for dz in (1, 0):
-                zz = pair * 2 + (z + dz) % 2
-                for dy in (1, 0):
-                    if dz or dy:
-                        to_owner(s, h, zz, (yl + dy) % 2).start()
-                    else:
-
-                        @pl.when(it == 0)
-                        def _():
-                            to_owner(s, h, zz, yl).start()
+
+            @pl.when(it == 0)
+            def _():
+                for b in range(4):
+                    to_owner(s, h, pair * 2 + b // 2, b % 2, 0).start()
 
             return 0
 
         lax.fori_loop(0, 2, mine, 0)
-
-    def finish(s, h):
-        total = col_out[s, h, z * 2 + yl]
+        last = [(z // 2 * 2 + (z + 1) % 2, 1 - yl), (z // 2 * 2 + (z + 1) % 2, yl), (z, 1 - yl)]
+        first = [((z // 2 * 2 + 2 + b // 2) % 4, b % 2) for b in range(4)]
+        for zz, yy in last:
+            to_owner(s, h, zz, yy, 0).start()
+        for k in range(1, CHUNKS):
+            for zz, yy in first + last:
+                to_owner(s, h, zz, yy, k).start()
+
+    def finish(s, h, k):
+        rows = rows_of(k)
+        total = col_out[s, h, z * 2 + yl, rows]
         for slot, mate in col_mates:
-            from_mate(s, h, slot, mate).wait_recv()
-            total = total + col_in[s, h, slot]
-        new = jnp.tanh(RETAIN * total * inv_ref[...] + TELEPORT * psrc_ref[h])
+            from_mate(s, h, slot, mate, k).wait_recv()
+            total = total + col_in[s, h, slot, rows]
+        new = jnp.tanh(RETAIN * total * inv_ref[rows] + TELEPORT * psrc_ref[h, rows])
         if s < STEPS - 1:
-            x_ref[s + 1, h, row] = new
-            for copy in spread(s + 1, h):
+            x_ref[s + 1, h, row, rows] = new
+            for copy in spread(s + 1, h, k):
                 copy.start()
         else:
-            last_ref[h] = new
+            last_ref[h, rows] = new
 
     pass_on(0, 0)
     e_sib.start()
@@ -339,19 +342,23 @@
         multiply_near(s, 1)
         if s == 0:
             take_energy()
-        multiply_far(s, 1)
         if s < STEPS - 1:
-            finish(s, 0)
+            finish(s, 0, 0)
+            multiply_far(s, 1)
+            finish(s, 0, 1)
             join(s, 1)
             pass_on(s + 1, 0)
             multiply_near(s + 1, 0)
+            finish(s, 1, 0)
             multiply_far(s + 1, 0)
-            finish(s, 1)
+            finish(s, 1, 1)
             join(s + 1, 0)
         else:
+            multiply_far(s, 1)
             join(s, 1)
-            finish(s, 0)
-            finish(s, 1)
+            for h in range(2):
+                for k in range(CHUNKS):
+                    finish(s, h, k)
 
     left, right = last_ref[0], last_ref[1]
     out_ref[0:128] = jnp.where(low, left, pltpu.roll(right, 64, 1))
@@ -361,12 +368,14 @@
         e_mate(slot, mate, slot).wait_send()
     for s in range(STEPS):
         for h in range(2):
-            for copy in spread(s, h) + forward(s, h):
-                copy.wait_send()
+            for k in range(CHUNKS):
+                for copy in spread(s, h, k) + forward(s, h, k):
+                    copy.wait_send()
             for pair in range(2):
                 to_sibling(s, h, pair).wait_send()
             for slot, mate in col_mates:
-                from_mate(s, h, slot, mate).wait_send()
+                for k in range(CHUNKS):
+                    from_mate(s, h, slot, mate, k).wait_send()
 
 
 def shards(source, value, occupancy, exponent):
@@ -403,9 +412,9 @@
             VMEM((8, 8, 256), F32),
             VMEM((2, 128, 128), F32),
             dma((16,)),
-            dma((*halves, 12)), dma((*halves, 8)),
+            dma((*halves, 12, CHUNKS)), dma((*halves, 8, CHUNKS)),
             dma((*halves, 2)), dma((*halves, 2)),
-            dma((*halves, 8)), dma((*halves, 8)),
+            dma((*halves, 8, CHUNKS)), dma((*halves, 8, CHUNKS)),
             dma, dma,
             dma((8,)), dma((8,)),
         ],

time: 87.9 us -> 85.4 us (0.972)
  Pallas kernels: 86.2 us -> 83.7 us
    pallas_call x1, Pallas kernels: 86.2 us -> 83.7 us  [shards(): pl.pallas_call(kernel, out_shape=jax.ShapeDtypeStruct((256, 128), F32), i...]
where the time goes in v3:
time: 85.4 us; the launch traced here: 85.3 us
  Pallas kernels  83.7 us (98%)
  local copies, waits for them, and re-layouts  1.57 us (2%)
    pallas_call x1, Pallas kernels, shards(): pl.pallas_call(kernel, out_shape=jax.ShapeDtypeStruct((256, 128), F32), i...  83.7 us

profile of v3, /device:TPU:1, one launch (start us, length us, event | category | flops | bytes accessed | tf_op | source)
XLA Modules:
  0.0 85.3 jit_solution(17168596203671689904)
XLA Ops:
  0.0 83.7 %shard_map.46 = f32[256,128]{1,0:T(8,128)} custom-call(f32[256,128]{1,0:T(8,128)} %src_hbm.1, bf16[4096,2048]{1,0:T(8,128)(2,1)} %val_ref.1, s32[16,32]{1,0:T(8,128)} %bitcast.2, s32[16,32]{1,0:T(8,128)} %bitcast.3), custom_call_target="tpu_custom_call" | custom-call | flops 12884901888 | bytes 17825792 | tf_op jit(solution)/shard_map/pallas_call | solution.py:385
  83.7 1.6 %copy.6 = f32[256,128]{1,0:T(8,128)} copy(f32[256,128]{1,0:T(8,128)} %shard_map.46) | data formatting | bytes 262144

commit v4 on v3

--- a/solution.py
+++ b/solution.py
@@ -104,11 +104,11 @@
 
     def spread(s, h, k):
         mates = [partner] + [yh * 4 + (x + dx) % 4 for dx in (1, 3, 2)]
-        mates += [(1 - yh) * 4 + (x + dx) % 4 for dx in (2, 1, 3) if s == 0 or dx not in FORWARDED]
+        mates += [(1 - yh) * 4 + (x + dx) % 4 for dx in (2, 1, 3) if (s, h) == (0, 0) or dx not in FORWARDED]
         return [gather_copy(s, h, row, k, mate, mate) for mate in mates]
 
     def forward(s, h, k):
-        if s == 0:
+        if (s, h) == (0, 0):
             return []
         return [
             gather_copy(s, h, partner, k, 8 + dx, yh * 4 + (x + dx) % 4) for dx in FORWARDED
@@ -260,14 +260,14 @@
             load_rhs(s, h, a)
 
         def tile(m, _):
-            rows = pl.ds(pl.multiple_of(m * 1024, 1024), 1024)
+            rows = pl.ds(pl.multiple_of(m * 2048, 2048), 2048)
             acc_ref[rows, :] = jnp.dot(
                 a_ref[rows, 0:1280], rhs_ref[0:1280, :],
                 preferred_element_type=F32,
             )
             return 0
 
-        lax.fori_loop(0, 4, tile, 0)
+        lax.fori_loop(0, 2, tile, 0)
 
     def far_tile(whose, pair):
         rows = pl.ds(pl.multiple_of(whose * 2048 + pair * 1024, 1024), 1024)
@@ -384,7 +384,7 @@
     halves = (STEPS, 2)
     return pl.pallas_call(
         kernel,
-        out_shape=jax.ShapeDtypeStruct((256, 128), F32),
+        out_shape=pltpu.VMEM((256, 128), F32),
         in_specs=[pl.BlockSpec(memory_space=pltpu.HBM)] * 4,
         out_specs=vmem,
         scratch_shapes=[

time: 85.4 us -> 83.2 us (0.974)
  Pallas kernels: 83.7 us -> 82.4 us
  local copies, waits for them, and re-layouts: 1.57 us -> 0.66 us
    pallas_call x1, Pallas kernels: 83.7 us -> 82.4 us  [shards(): pl.pallas_call(kernel, out_shape=pltpu.VMEM((256, 128), F32), in_specs=[p...]
    unnamed x1, local copies, waits for them, and re-layouts: 1.57 us -> 0.66 us
where the time goes in v4:
time: 83.2 us; the launch traced here: 83.1 us
  Pallas kernels  82.4 us (99%)
    pallas_call x1, Pallas kernels, shards(): pl.pallas_call(kernel, out_shape=pltpu.VMEM((256, 128), F32), in_specs=[p...  82.4 us

profile of v4, /device:TPU:1, one launch (start us, length us, event | category | flops | bytes accessed | tf_op | source)
XLA Modules:
  0.0 83.1 jit_solution(3018235126990088083)
XLA Ops:
  0.0 82.4 %shard_map.46 = f32[256,128]{1,0:T(8,128)S(1)} custom-call(f32[256,128]{1,0:T(8,128)} %src_hbm.1, bf16[4096,2048]{1,0:T(8,128)(2,1)} %val_ref.1, s32[16,32]{1,0:T(8,128)} %bitcast.2, s32[16,32]{1,0:T(8,128)} %bitcast.3), custom_call_target="tpu_custom_call" | custom-call | flops 12884901888 | bytes 17825792 | tf_op jit(solution)/shard_map/pallas_call | solution.py:385
  82.5 0.7 copy.6

commit v5 on v4

--- a/solution.py
+++ b/solution.py
@@ -334,8 +334,8 @@
     pass_on(0, 0)
     e_sib.start()
     multiply_near(0, 0)
+    send_energy()
     multiply_far(0, 0)
-    send_energy()
     join(0, 0)
     for s in range(STEPS):
         pass_on(s, 1)

time: 83.2 us -> 83.1 us (level)
  no operation moved by 1% of the time
where the time goes in v5:
time: 83.1 us; the launch traced here: 83 us
  Pallas kernels  82.3 us (99%)
    pallas_call x1, Pallas kernels, shards(): pl.pallas_call(kernel, out_shape=pltpu.VMEM((256, 128), F32), in_specs=[p...  82.3 us

profile of v5, /device:TPU:1, one launch (start us, length us, event | category | flops | bytes accessed | tf_op | source)
XLA Modules:
  0.0 83.0 jit_solution(13903693808746496880)
XLA Ops:
  0.0 82.3 %shard_map.46 = f32[256,128]{1,0:T(8,128)S(1)} custom-call(f32[256,128]{1,0:T(8,128)} %src_hbm.1, bf16[4096,2048]{1,0:T(8,128)(2,1)} %val_ref.1, s32[16,32]{1,0:T(8,128)} %bitcast.2, s32[16,32]{1,0:T(8,128)} %bitcast.3), custom_call_target="tpu_custom_call" | custom-call | flops 12884901888 | bytes 17825792 | tf_op jit(solution)/shard_map/pallas_call | solution.py:385
  82.3 0.7 copy.6
